TPU v7x, 512 devices: a whole 4x4x16 slice. The times are simulated.
512 devices in a mesh: chan: 64 (over z, y), rad: 8 (over x, core).
Axes of the slice: x: 4, y: 4, z: 16, core: 2. Of those that a mesh axis runs over, the one named last changes fastest.
Arguments:
- trial_block: float32 [1024, 16, 128], P('chan', None, 'rad')
- ham_blocks: bfloat16 [1024, 8, 128, 128], P('chan', None, 'rad'), may hold values from -0.1875 to 0.1875
- partners: int32 [1024, 8], P('chan'), may hold values from 0 to 1023, as said below
- stored_at: int32 [1024], replicated, may hold values from 0 to 1023, as said below
- precond_diag: float32 [1024, 128], P('chan', 'rad'), may hold values from 1 to 10
Outputs:
- new_block: float32 [1024, 16, 128], P('chan', None, 'rad')
- ritz_values: float32 [16], replicated
Inputs may be any that keep to these rules, and one draw needn't show every extreme that they name: `stored_at`: A permutation of the channel numbers. `partners`: among the 128 entries of the rows p with p // 16 = d, for every d, at most 4 have stored_at[partner] // 16 equal to any one value; for every d some value has exactly 4.
All inputs are finite; a program needn't handle non-finite values.
Results may differ from a plain program's by a relative error of at most 0.0051.
Values may be sent and summed in bfloat16 or wider, within the bound.
A program may use at most 64 MiB of HBM per device.

v0:
```python
import jax
import jax.numpy as jnp
from jax import lax
from jax.sharding import PartitionSpec as P

NCH = 1024
NB = 128


def chol_solve(factor, rhs):
    first = lax.linalg.triangular_solve(factor, rhs, left_side=True, lower=True)
    return lax.linalg.triangular_solve(factor, first, left_side=True, lower=True, transpose_a=True)


def inner_products(left, right):
    return jnp.einsum("pkr,plr->kl", left, right, precision=lax.Precision.HIGHEST)


def body(trial_block, ham_blocks, partners, stored_at, precond_diag):
    n_chan = lax.axis_size("chan")
    ch_dev = trial_block.shape[0]
    vectors = trial_block.shape[1]
    ncoup = partners.shape[1]
    capacity = 2 * ch_dev * ncoup // n_chan
    stored_rows = jnp.take(stored_at, partners.reshape(-1))
    owner_dev = stored_rows // ch_dev
    local_row = stored_rows % ch_dev
    one_hot = (owner_dev[:, None] == jnp.arange(n_chan, dtype=jnp.int32)[None, :]).astype(jnp.int32)
    running = jnp.cumsum(one_hot, axis=0)
    order_rank = jnp.sum(running * one_hot, axis=1) - 1
    slot_index = owner_dev * capacity + order_rank
    wanted = (
        jnp.zeros((n_chan * capacity,), jnp.int32)
        .at[slot_index]
        .set(local_row)
        .reshape(n_chan, capacity)
    )
    asked = lax.all_to_all(wanted, "chan", split_axis=0, concat_axis=0, tiled=True)
    rounded = trial_block.astype(jnp.bfloat16)
    whole_rows = lax.all_gather(rounded, "rad", axis=2, tiled=True)
    served = whole_rows[asked]
    received = lax.all_to_all(served, "chan", split_axis=0, concat_axis=0, tiled=True)
    full_splines = received.shape[3]
    coupled = received.reshape(n_chan * capacity, vectors, full_splines)[slot_index]
    coupled = coupled.reshape(ch_dev, ncoup, vectors, full_splines)
    applied = lax.dot_general(
        coupled, ham_blocks, (((1, 3), (1, 3)), ((0,), (0,))), preferred_element_type=jnp.float32
    )
    total_rows = jnp.float32(NCH * NB)
    proj_a, proj_b = lax.psum(
        (inner_products(trial_block, applied), inner_products(trial_block, trial_block)),
        ("chan", "rad"),
    )
    factor = jnp.linalg.cholesky(proj_b)
    coefficients = chol_solve(factor, proj_a)
    ritz_values = jnp.diagonal(coefficients)
    residual = applied - jnp.einsum(
        "pkr,kl->plr", trial_block, coefficients, precision=lax.Precision.HIGHEST
    )
    correction = residual / precond_diag[:, None, :]
    correlation = lax.psum(inner_products(trial_block, correction), ("chan", "rad"))
    mixing = chol_solve(factor, correlation)
    projected = correction - jnp.einsum(
        "pkr,kl->plr", trial_block, mixing, precision=lax.Precision.HIGHEST
    )
    correlation_gram = lax.psum(inner_products(projected, projected), ("chan", "rad")) / total_rows
    gram_factor = jnp.linalg.cholesky(correlation_gram)
    local_splines = projected.shape[2]
    flat_rows = jnp.transpose(projected, (1, 0, 2)).reshape(vectors, -1)
    solved = lax.linalg.triangular_solve(gram_factor, flat_rows, left_side=True, lower=True)
    new_block = jnp.transpose(solved.reshape(vectors, ch_dev, local_splines), (1, 0, 2))
    return (new_block, ritz_values)


def solution(mesh):
    return jax.shard_map(
        body,
        mesh=mesh,
        in_specs=(
            P("chan", None, "rad"),
            P("chan", None, "rad", None),
            P("chan", None),
            P(),
            P("chan", "rad"),
        ),
        out_specs=(P("chan", None, "rad"), P()),
        check_vma=False,
    )
```

profile of v0, /device:TPU:1, one launch (start us, length us, event | category | flops | bytes accessed | tf_op | source)
XLA Modules:
  0.0 426.4 jit_solution(2646082566353192529)
XLA Ops:
  0.6 0.8 copy.36
  1.7 0.7 copy-done.1
  2.3 1.0 gather_fusion
  3.8 1.0 scatter_custom_fusion
  4.8 0.7 all_to_all.11
  5.5 19.3 %all-to-all-start = ((s32[64,1,4]{2,1,0:T(1,128)}), s32[64,1,4]{2,1,0:T(1,128)S(1)}, u32[]{:S(2)}, u32[]{:S(2)}) async-start(s32[64,1,4]{2,1,0:T(1,128)} %bitcast.4), calls=%async_computation | async-start | bytes 65536 | tf_op jit(solution)/shard_map/all_to_all | solution.py:38
  24.9 14.3 %all_gather.3 = bf16[16,16,128]{1,0,2:T(8,128)(2,1)S(1)} all-gather(bf16[16,16,16]{1,0,2:T(8,128)(2,1)S(1)} %copy.35), channel_id=1, replica_groups=mesh['chan'=64,'rad'=8] {'rad'}, dimensions={2}, use_global_device_ids=true | all-gather | bytes 73728 | tf_op jit(solution)/shard_map/all_gather | solution.py:40
  39.8 1.8 gather_fusion.1
  41.5 14.8 %all-to-all-start.1 = ((bf16[64,4,16,128]{3,2,1,0:T(8,128)(2,1)}), bf16[64,4,16,128]{3,2,1,0:T(8,128)(2,1)S(1)}, u32[]{:S(2)}, u32[]{:S(2)}) async-start(bf16[64,4,16,128]{3,2,1,0:T(8,128)(2,1)} %bitcast.6), calls=%async_computation.1 | async-start | bytes 2097152 | tf_op jit(solution)/shard_map/all_to_all | solution.py:42
  56.6 52.5 %all-to-all-done.1 = bf16[64,4,16,128]{3,2,1,0:T(8,128)(2,1)S(1)} async-done(((bf16[64,4,16,128]{3,2,1,0:T(8,128)(2,1)}), bf16[64,4,16,128]{3,2,1,0:T(8,128)(2,1)S(1)}, u32[]{:S(2)}, u32[]{:S(2)}) %all-to-all-start.1) | async-done | bytes 1048608 | tf_op jit(solution)/shard_map/all_to_all | solution.py:42
  109.2 0.7 gather_fusion.2
  110.4 103.4 %all-reduce = (f32[16,16]{0,1:T(8,128)S(1)}, f32[16,16]{0,1:T(8,128)S(1)}) all-reduce(f32[16,16]{0,1:T(8,128)S(1)} %convolution_bitcast_fusion.4, f32[16,16]{0,1:T(8,128)S(1)} %convolution_bitcast_fusion.5), channel_id=1, replica_groups=mesh['chan'=64,'rad'=8] {'chan','rad'}, use_global_device_ids=true, to_apply=%region_6.8 | all-reduce | flops 512 | bytes 4096 | tf_op jit(solution)/shard_map/psum | solution.py:50
  213.9 1.5 cholesky.44
  215.4 0.6 compare_reduce_fusion.1
  216.0 0.6 fusion.5
  216.7 1.2 custom-call.17
  219.3 99.6 %psum.30 = f32[16,16]{0,1:T(8,128)S(1)} all-reduce(f32[16,16]{0,1:T(8,128)S(1)} %convolution_bitcast_fusion.3), channel_id=1, replica_groups=mesh['chan'=64,'rad'=8] {'chan','rad'}, use_global_device_ids=true, to_apply=%region_7.11 | all-reduce | flops 256 | bytes 2048 | tf_op jit(solution)/shard_map/psum | solution.py:61
  319.8 99.4 %psum.31 = f32[16,16]{0,1:T(8,128)S(1)} all-reduce(f32[16,16]{0,1:T(8,128)S(1)} %convolution_bitcast_fusion.1), channel_id=1, replica_groups=mesh['chan'=64,'rad'=8] {'chan','rad'}, use_global_device_ids=true, to_apply=%region_8.12 | all-reduce | flops 256 | bytes 2048 | tf_op jit(solution)/shard_map/psum | solution.py:66
  419.2 1.5 cholesky.55
  420.7 0.6 compare_reduce_fusion
  421.4 0.6 fusion.6
  422.0 1.2 custom-call.11
  423.5 1.2 gather_fusion.3
  424.7 1.7 convolution_bitcast_fusion
  (46 shorter events, 4.9 us)
Async XLA Ops:
  0.6 109.2 %copy-start = (bf16[16,8,16,128]{3,2,1,0:T(8,128)(2,1)S(1)}, bf16[16,8,16,128]{3,2,1,0:T(8,128)(2,1)}, u32[]{:S(2)}) copy-start(bf16[16,8,16,128]{3,2,1,0:T(8,128)(2,1)} %param.11) | copy-start | bytes 1572868
  1.6 0.7 copy-start.1
  3.4 21.4 %copy-start.2 = (f32[16,16,16]{2,1,0:T(8,128)S(1)}, f32[16,16,16]{2,1,0:T(8,128)}, u32[]{:S(2)}) copy-start(f32[16,16,16]{2,1,0:T(8,128)} %param.10) | copy-start | bytes 49156
  5.5 34.1 %all-to-all-start = ((s32[64,1,4]{2,1,0:T(1,128)}), s32[64,1,4]{2,1,0:T(1,128)S(1)}, u32[]{:S(2)}, u32[]{:S(2)}) async-start(s32[64,1,4]{2,1,0:T(1,128)} %bitcast.4), calls=%async_computation | async-start | bytes 65536 | tf_op jit(solution)/shard_map/all_to_all | solution.py:38
  41.5 67.6 %all-to-all-start.1 = ((bf16[64,4,16,128]{3,2,1,0:T(8,128)(2,1)}), bf16[64,4,16,128]{3,2,1,0:T(8,128)(2,1)S(1)}, u32[]{:S(2)}, u32[]{:S(2)}) async-start(bf16[64,4,16,128]{3,2,1,0:T(8,128)(2,1)} %bitcast.6), calls=%async_computation.1 | async-start | bytes 2097152 | tf_op jit(solution)/shard_map/all_to_all | solution.py:42
  218.3 0.7 copy-start.3
where the time goes:
time: 427 us; the launch traced here: 426 us
  blocking collectives  317 us (74%)
  waiting for transfers between devices  52.5 us (12%)
  starting transfers between devices  34.1 us (8%)
  local copies, waits for them, and re-layouts  9.41 us (2%)
  other arithmetic  8.53 us (2%)
  matrix products  4.37 us (1%)
    psum x1, blocking collectives, body(): lax.psum((inner_products(trial_block, applied), inner_products(trial_bloc...  103 us
    psum x1, blocking collectives, body(): lax.psum(inner_products(trial_block, correction), ('chan', 'rad'))  99.6 us
    psum x1, blocking collectives, body(): lax.psum(inner_products(projected, projected), ('chan', 'rad')) / total_rows  99.4 us
    all_to_all x1, waiting for transfers between devices, body(): lax.all_to_all(served, 'chan', split_axis=0, concat_axis=0, tiled=True)  52.5 us
    all_to_all x1, starting transfers between devices, body(): lax.all_to_all(wanted, 'chan', split_axis=0, concat_axis=0, tiled=True)  19.3 us
    all_to_all x1, starting transfers between devices, body(): lax.all_to_all(served, 'chan', split_axis=0, concat_axis=0, tiled=True)  14.8 us
    all_gather x1, blocking collectives, body(): whole_rows = lax.all_gather(rounded, 'rad', axis=2, tiled=True)  14.3 us
  transfers between devices with their start and end apart: 2, of which 1 were waited for; matrix products, arithmetic and copies ran while one was open for 0% of the time, Pallas kernels for 0%

commit v1 on v0

--- a/solution.py
+++ b/solution.py
@@ -63,7 +63,10 @@
     projected = correction - jnp.einsum(
         "pkr,kl->plr", trial_block, mixing, precision=lax.Precision.HIGHEST
     )
-    correlation_gram = lax.psum(inner_products(projected, projected), ("chan", "rad")) / total_rows
+    correlation_gram = (
+        jnp.sum(lax.all_gather(inner_products(projected, projected), ("chan", "rad")), axis=0)
+        / total_rows
+    )
     gram_factor = jnp.linalg.cholesky(correlation_gram)
     local_splines = projected.shape[2]
     flat_rows = jnp.transpose(projected, (1, 0, 2)).reshape(vectors, -1)

time: 427 us -> 474 us (1.11)
  blocking collectives: 317 us -> 360 us
    all_gather x0 -> x1, blocking collectives: none -> 143 us  [body(): lax.all_gather(inner_products(projected, projected), ('chan', 'rad'))]
    psum x1 -> x0, blocking collectives: 99.4 us -> none  [body(): lax.psum(inner_products(projected, projected), ('chan', 'rad')) / total_rows]
where the time goes in v1:
time: 474 us; the launch traced here: 473 us
  blocking collectives  360 us (76%)
  waiting for transfers between devices  52.5 us (11%)
  starting transfers between devices  34.1 us (7%)
  other arithmetic  11.3 us (2%)
  local copies, waits for them, and re-layouts  10.1 us (2%)
    all_gather x1, blocking collectives, body(): lax.all_gather(inner_products(projected, projected), ('chan', 'rad'))  143 us
    psum x1, blocking collectives, body(): lax.psum((inner_products(trial_block, applied), inner_products(trial_bloc...  103 us
    psum x1, blocking collectives, body(): lax.psum(inner_products(trial_block, correction), ('chan', 'rad'))  99.6 us
    all_to_all x1, waiting for transfers between devices, body(): lax.all_to_all(served, 'chan', split_axis=0, concat_axis=0, tiled=True)  52.5 us
    all_to_all x1, starting transfers between devices, body(): lax.all_to_all(wanted, 'chan', split_axis=0, concat_axis=0, tiled=True)  19.3 us
    all_to_all x1, starting transfers between devices, body(): lax.all_to_all(served, 'chan', split_axis=0, concat_axis=0, tiled=True)  14.8 us
    all_gather x1, blocking collectives, body(): whole_rows = lax.all_gather(rounded, 'rad', axis=2, tiled=True)  14.3 us
  transfers between devices with their start and end apart: 2, of which 1 were waited for; matrix products, arithmetic and copies ran while one was open for 0% of the time, Pallas kernels for 0%

profile of v1, /device:TPU:1, one launch (start us, length us, event | category | flops | bytes accessed | tf_op | source)
XLA Modules:
  0.0 473.1 jit_solution(17779116125023116573)
XLA Ops:
  0.7 0.8 copy.34
  1.7 1.6 gather_fusion
  3.8 1.0 scatter_custom_fusion
  4.8 0.7 all_to_all.11
  5.5 19.3 %all-to-all-start = ((s32[64,1,4]{2,1,0:T(1,128)}), s32[64,1,4]{2,1,0:T(1,128)S(1)}, u32[]{:S(2)}, u32[]{:S(2)}) async-start(s32[64,1,4]{2,1,0:T(1,128)} %bitcast.4), calls=%async_computation | async-start | bytes 65536 | tf_op jit(solution)/shard_map/all_to_all | solution.py:38
  24.8 1.0 copy.33
  25.8 14.3 %all_gather.9 = bf16[16,16,128]{1,0,2:T(8,128)(2,1)S(1)} all-gather(bf16[16,16,16]{1,0,2:T(8,128)(2,1)S(1)} %copy.33), channel_id=1, replica_groups=mesh['chan'=64,'rad'=8] {'rad'}, dimensions={2}, use_global_device_ids=true | all-gather | bytes 73728 | tf_op jit(solution)/shard_map/all_gather | solution.py:40
  40.6 1.8 gather_fusion.1
  42.4 14.8 %all-to-all-start.1 = ((bf16[64,4,16,128]{3,2,1,0:T(8,128)(2,1)}), bf16[64,4,16,128]{3,2,1,0:T(8,128)(2,1)S(1)}, u32[]{:S(2)}, u32[]{:S(2)}) async-start(bf16[64,4,16,128]{3,2,1,0:T(8,128)(2,1)} %bitcast.6), calls=%async_computation.1 | async-start | bytes 2097152 | tf_op jit(solution)/shard_map/all_to_all | solution.py:42
  57.5 52.5 %all-to-all-done.1 = bf16[64,4,16,128]{3,2,1,0:T(8,128)(2,1)S(1)} async-done(((bf16[64,4,16,128]{3,2,1,0:T(8,128)(2,1)}), bf16[64,4,16,128]{3,2,1,0:T(8,128)(2,1)S(1)}, u32[]{:S(2)}, u32[]{:S(2)}) %all-to-all-start.1) | async-done | bytes 1048608 | tf_op jit(solution)/shard_map/all_to_all | solution.py:42
  110.0 0.7 gather_fusion.2
  111.3 103.4 %all-reduce = (f32[16,16]{0,1:T(8,128)S(1)}, f32[16,16]{0,1:T(8,128)S(1)}) all-reduce(f32[16,16]{0,1:T(8,128)S(1)} %convolution_bitcast_fusion.4, f32[16,16]{0,1:T(8,128)S(1)} %convolution_bitcast_fusion.5), channel_id=1, replica_groups=mesh['chan'=64,'rad'=8] {'chan','rad'}, use_global_device_ids=true, to_apply=%region_6.8 | all-reduce | flops 512 | bytes 4096 | tf_op jit(solution)/shard_map/psum | solution.py:50
  214.8 1.5 cholesky.44
  216.3 0.6 compare_reduce_fusion.1
  216.9 0.6 fusion.5
  217.6 1.2 custom-call.17
  219.5 1.2 gather_fusion.3
  220.9 99.6 %psum.23 = f32[16,16]{0,1:T(8,128)S(1)} all-reduce(f32[16,16]{0,1:T(8,128)S(1)} %convolution_bitcast_fusion.3), channel_id=1, replica_groups=mesh['chan'=64,'rad'=8] {'chan','rad'}, use_global_device_ids=true, to_apply=%region_7.11 | all-reduce | flops 256 | bytes 2048 | tf_op jit(solution)/shard_map/psum | solution.py:61
  321.8 142.7 %all-gather = f32[8192,16]{1,0:T(8,128)} all-gather(f32[16,16]{1,0:T(8,128)S(1)} %convolution_bitcast_fusion.1), channel_id=2, replica_groups=mesh['chan'=64,'rad'=8] {'chan','rad'}, dimensions={0}, use_global_device_ids=true | all-gather | bytes 525312 | tf_op jit(solution)/shard_map/all_gather | solution.py:67
  464.5 2.7 reduce_sum.19
  467.4 1.5 cholesky.55
  469.5 0.6 fusion.6
  470.1 1.2 custom-call.11
  471.4 1.7 convolution_bitcast_fusion
  (46 shorter events, 5.2 us)
Async XLA Ops:
  0.6 110.1 %copy-start = (bf16[16,8,16,128]{3,2,1,0:T(8,128)(2,1)S(1)}, bf16[16,8,16,128]{3,2,1,0:T(8,128)(2,1)}, u32[]{:S(2)}) copy-start(bf16[16,8,16,128]{3,2,1,0:T(8,128)(2,1)} %param.11) | copy-start | bytes 1572868
  0.6 56.6 %copy-start.1 = (f32[16,16,16]{2,1,0:T(8,128)S(1)}, f32[16,16,16]{2,1,0:T(8,128)}, u32[]{:S(2)}) copy-start(f32[16,16,16]{2,1,0:T(8,128)} %param.10) | copy-start | bytes 49156
  5.5 35.0 %all-to-all-start = ((s32[64,1,4]{2,1,0:T(1,128)}), s32[64,1,4]{2,1,0:T(1,128)S(1)}, u32[]{:S(2)}, u32[]{:S(2)}) async-start(s32[64,1,4]{2,1,0:T(1,128)} %bitcast.4), calls=%async_computation | async-start | bytes 65536 | tf_op jit(solution)/shard_map/all_to_all | solution.py:38
  40.1 180.6 %copy-start.2 = (f32[16,16]{1,0:T(8,128)S(1)}, f32[16,16]{1,0:T(8,128)}, u32[]{:S(2)}) copy-start(f32[16,16]{1,0:T(8,128)} %param.14) | copy-start | bytes 3076
  42.4 67.6 %all-to-all-start.1 = ((bf16[64,4,16,128]{3,2,1,0:T(8,128)(2,1)}), bf16[64,4,16,128]{3,2,1,0:T(8,128)(2,1)S(1)}, u32[]{:S(2)}, u32[]{:S(2)}) async-start(bf16[64,4,16,128]{3,2,1,0:T(8,128)(2,1)} %bitcast.6), calls=%async_computation.1 | async-start | bytes 2097152 | tf_op jit(solution)/shard_map/all_to_all | solution.py:42
